TPU v7x, 32 devices: a whole 2x2x4 slice. The times are simulated.
32 devices in a mesh: wide: 8 (over z, y), narrow: 4 (over x, core).
Axes of the slice: x: 2, y: 2, z: 4, core: 2. Of those that a mesh axis runs over, the one named last changes fastest.
Arguments:
- tokens: bfloat16 [4, 4096, 1024], P('narrow', 'wide'), may hold values from -6 to 6
- cotangent: bfloat16 [4, 4096, 1024], P('narrow', 'wide'), may hold values from -6 to 6
- lengths: int32 [4, 16], P('narrow'), may hold values from 0 to 4095, as said below
- decay_rate: float32 [8], replicated, may hold values from 0 to 0.034, as said below
- attn_gain: float32 [1024], replicated, may hold values from 0.1 to 1.9
- w_query: bfloat16 [1024, 1024], replicated, may hold values from -0.1875 to 0.1875
- w_key: bfloat16 [1024, 1024], replicated, may hold values from -0.1875 to 0.1875
- w_value: bfloat16 [1024, 1024], replicated, may hold values from -0.1875 to 0.1875
- w_gate: bfloat16 [1024, 1024], replicated, may hold values from -0.1875 to 0.1875
- w_out: bfloat16 [1024, 1024], replicated, may hold values from -0.1875 to 0.1875
- ffn_gain: float32 [1024], replicated, may hold values from 0.1 to 1.9
- w_left: bfloat16 [1024, 2816], P(None, 'narrow'), may hold values from -0.1875 to 0.1875
- w_right: bfloat16 [1024, 2816], P(None, 'narrow'), may hold values from -0.1875 to 0.1875
- w_down: bfloat16 [2816, 1024], P('narrow'), may hold values from -0.109375 to 0.109375
Outputs:
- output: bfloat16 [4, 4096, 1024], P('narrow', 'wide')
- grad_tokens: float32 [4, 4096, 1024], P('narrow', 'wide')
- grad_w_query: float32 [1024, 1024], replicated
- grad_w_key: float32 [1024, 1024], replicated
- grad_w_value: float32 [1024, 1024], replicated
- grad_w_gate: float32 [1024, 1024], replicated
- grad_w_out: float32 [1024, 1024], replicated
- grad_attn_gain: float32 [1024], replicated
- grad_ffn_gain: float32 [1024], replicated
- grad_w_left: float32 [1024, 2816], P(None, 'narrow')
- grad_w_right: float32 [1024, 2816], P(None, 'narrow')
- grad_w_down: float32 [2816, 1024], P('narrow')
Inputs may be any that keep to these rules, and one draw needn't show every extreme that they name: lengths[r] holds the lengths of pack r's sequences in order, then zeros for unused slots; every pack closes with 1 to 255 padding positions; one pack holds a single sequence of 4095 positions. One position's decay of head h is exp(-decay_rate[h]).
All inputs are finite; a program needn't handle non-finite values.
Results may differ from a plain program's by a relative error of at most 0.019.
Values may be sent and summed in bfloat16 or wider, within the bound.
A program may use at most 192 MiB of HBM per device.

v0:
```python
import jax
import jax.numpy as jnp
from jax import lax
from jax.sharding import PartitionSpec as P

EPS = 1e-06
HIGH = lax.Precision.HIGHEST


def carried_in(array, axis, join, neutral, backward):
    count = lax.axis_size(axis)
    place = lax.axis_index(axis)
    ahead = count - 1 - place if backward else place
    gathered = jax.tree.map(
        lambda a, kind: lax.all_gather(a.astype(kind), axis), array, (jnp.bfloat16, jnp.bfloat16)
    )
    state = jax.tree.map(lambda a, e: jnp.zeros_like(a) + jnp.asarray(e, a.dtype), array, neutral)

    def one(hop, state):
        source = count - 1 - hop if backward else hop
        return join(
            state,
            jax.tree.map(
                lambda a, own: lax.dynamic_index_in_dim(a, source, 0, False).astype(own.dtype),
                gathered,
                array,
            ),
        )

    return lax.fori_loop(0, ahead, one, state)


def rms_scale(vector):
    return vector * lax.rsqrt(jnp.mean(vector * vector, axis=-1, keepdims=True) + EPS)


def scale_norm(vector, gain):
    return rms_scale(vector) * gain


def contract_rows(left_mat, right_mat):
    return lax.dot_general(
        left_mat, right_mat, (((0,), (0,)), ((), ())), preferred_element_type=jnp.float32
    )


def times_transpose(left_mat, right_mat):
    return lax.dot_general(
        left_mat, right_mat, (((1,), (1,)), ((), ())), preferred_element_type=jnp.float32
    )


def combine_affine(earlier, later):
    return (earlier[0] * later[0], later[0][:, None, None] * earlier[1] + later[1])


def body(
    tokens,
    cotangent,
    lengths,
    decay_rate,
    attn_gain,
    w_query,
    w_key,
    w_value,
    w_gate,
    w_out,
    ffn_gain,
    w_left,
    w_right,
    w_down,
):
    rows_dev = tokens.shape[1]
    model_width = tokens.shape[2]
    num_heads = decay_rate.shape[0]
    head_dim = model_width // num_heads
    f32 = jnp.float32
    bf16 = jnp.bfloat16
    inputs = tokens[0].astype(f32)
    anchor = lax.axis_index("wide") * rows_dev
    seq_ends = jnp.cumsum(lengths[0])
    places = anchor + jnp.arange(-1, rows_dev)
    segment_all = jnp.sum((places[:, None] >= seq_ends[None, :]).astype(jnp.int32), axis=1)
    segment = segment_all[1:]
    is_live = places[1:] < seq_ends[-1]
    seg_prev = jnp.where(anchor > 0, segment_all[0], -1)
    seg_last = segment[rows_dev - 1]
    local_pos = jnp.arange(rows_dev)
    offset = local_pos[:, None] - local_pos[None, :]
    causal = offset >= 0
    allowed = causal & (segment[:, None] == segment[None, :]) & is_live[:, None] & is_live[None, :]
    decay_mask = (
        jnp.exp(-decay_rate[:, None, None] * jnp.where(causal, offset, 0).astype(f32)[None])
        * allowed.astype(f32)[None]
    )
    gate_in = (
        jnp.exp(-decay_rate[:, None] * (local_pos + 1).astype(f32)[None])
        * ((segment == seg_prev) & is_live).astype(f32)[None]
    )
    keep_out = (
        jnp.exp(-decay_rate[:, None] * (rows_dev - 1 - local_pos).astype(f32)[None])
        * ((segment == seg_last) & is_live).astype(f32)[None]
    )
    pass_on = jnp.exp(-decay_rate * rows_dev) * (seg_last == seg_prev).astype(f32)
    identity = (jnp.ones((num_heads,), f32), jnp.zeros((num_heads, head_dim, head_dim), f32))
    head_shape = (rows_dev, num_heads, head_dim)
    normed_first, norm_back1 = jax.vjp(scale_norm, inputs, attn_gain)
    normed1 = normed_first.astype(bf16)
    q_pre = jnp.dot(normed1, w_query, preferred_element_type=f32)
    k_pre = jnp.dot(normed1, w_key, preferred_element_type=f32)
    query_full, query_back = jax.vjp(jax.nn.silu, q_pre)
    key_full, key_back = jax.vjp(jax.nn.silu, k_pre)
    query = query_full.astype(bf16).reshape(head_shape)
    keyed = key_full.astype(bf16).reshape(head_shape)
    value = jnp.dot(normed1, w_value, preferred_element_type=f32).astype(bf16).reshape(head_shape)
    gate_u = jnp.dot(normed1, w_gate, preferred_element_type=f32)
    scores = jnp.einsum("thd,shd->hts", query, keyed, preferred_element_type=f32)
    probs = (scores * decay_mask).astype(bf16)
    intra = jnp.einsum("hts,shd->thd", probs, value, preferred_element_type=f32)
    query_wide = query.astype(f32)
    keyed_wide = keyed.astype(f32)
    value_wide = value.astype(f32)
    local_state = jnp.einsum(
        "shd,she->hde", keyed_wide * keep_out.T[:, :, None], value_wide, precision=HIGH
    )
    state_in = carried_in((pass_on, local_state), "wide", combine_affine, identity, False)[1]
    inter = jnp.einsum("thd,hde->the", query_wide, state_in, precision=HIGH) * gate_in.T[:, :, None]
    attn_raw = intra + inter
    normed_o, head_back = jax.vjp(rms_scale, attn_raw)
    flat_o = normed_o.reshape(rows_dev, model_width)
    mixed = (flat_o * gate_u).astype(bf16)
    hidden = inputs + jnp.dot(mixed, w_out, preferred_element_type=f32)
    normed_second, norm_back2 = jax.vjp(scale_norm, hidden, ffn_gain)
    normed2 = normed_second.astype(bf16)
    rows_all = lax.all_gather(normed2, "narrow", axis=0, tiled=True)
    left_act = jnp.dot(rows_all, w_left, preferred_element_type=f32)
    right_act = jnp.dot(rows_all, w_right, preferred_element_type=f32)
    product = (left_act * right_act).astype(bf16)
    ffn_out = lax.psum_scatter(
        jnp.dot(product, w_down, preferred_element_type=f32).astype(jnp.bfloat16),
        "narrow",
        scatter_dimension=0,
        tiled=True,
    ).astype(jnp.float32)
    output = (hidden + ffn_out).astype(bf16)
    grad_out = cotangent[0]
    grad_all = lax.all_gather(grad_out, "narrow", axis=0, tiled=True)
    grad_wdown = contract_rows(product, grad_all)
    grad_prod = times_transpose(grad_all, w_down)
    grad_left = (grad_prod * right_act).astype(bf16)
    grad_right = (grad_prod * left_act).astype(bf16)
    grad_wleft = contract_rows(rows_all, grad_left)
    grad_wright = contract_rows(rows_all, grad_right)
    grad_normed2 = lax.psum_scatter(
        (times_transpose(grad_left, w_left) + times_transpose(grad_right, w_right)).astype(
            jnp.bfloat16
        ),
        "narrow",
        scatter_dimension=0,
        tiled=True,
    ).astype(jnp.float32)
    grad_hid_part, grad_gain_two = norm_back2(grad_normed2)
    grad_hidden = grad_out.astype(f32) + grad_hid_part
    grad_branch = grad_hidden.astype(bf16)
    grad_mixed = times_transpose(grad_branch, w_out)
    grad_gate = (grad_mixed * flat_o).astype(bf16)
    grad_flat = (grad_mixed * gate_u).reshape(head_shape)
    grad_attn = head_back(grad_flat)[0].astype(bf16)
    grad_attn_wide = grad_attn.astype(f32)
    grad_probs = jnp.einsum("thd,shd->hts", grad_attn, value, preferred_element_type=f32)
    grad_scores = (grad_probs * decay_mask).astype(bf16)
    local_back = jnp.einsum(
        "thd,the->hde", query_wide * gate_in.T[:, :, None], grad_attn_wide, precision=HIGH
    )
    state_out = carried_in((pass_on, local_back), "wide", combine_affine, identity, True)[1]
    grad_query = (
        jnp.einsum("hts,shd->thd", grad_scores, keyed, preferred_element_type=f32)
        + jnp.einsum("the,hde->thd", grad_attn_wide, state_in, precision=HIGH)
        * gate_in.T[:, :, None]
    )
    grad_key = (
        jnp.einsum("hts,thd->shd", grad_scores, query, preferred_element_type=f32)
        + jnp.einsum("hde,she->shd", state_out, value_wide, precision=HIGH) * keep_out.T[:, :, None]
    )
    grad_value = (
        jnp.einsum("hts,thd->shd", probs, grad_attn, preferred_element_type=f32)
        + jnp.einsum("hde,shd->she", state_out, keyed_wide, precision=HIGH) * keep_out.T[:, :, None]
    )
    grad_qpre = query_back(grad_query.reshape(rows_dev, model_width))[0].astype(bf16)
    grad_kpre = key_back(grad_key.reshape(rows_dev, model_width))[0].astype(bf16)
    grad_vpre = grad_value.reshape(rows_dev, model_width).astype(bf16)
    grad_normed1 = (
        times_transpose(grad_qpre, w_query)
        + times_transpose(grad_kpre, w_key)
        + times_transpose(grad_vpre, w_value)
        + times_transpose(grad_gate, w_gate)
    )
    grad_in_part, grad_gain_one = norm_back1(grad_normed1)
    grad_tokens = (grad_hidden + grad_in_part)[None]
    summed = lax.psum(
        (
            contract_rows(normed1, grad_qpre),
            contract_rows(normed1, grad_kpre),
            contract_rows(normed1, grad_vpre),
            contract_rows(normed1, grad_gate),
            contract_rows(mixed, grad_branch),
            grad_gain_one,
            grad_gain_two,
        ),
        ("wide", "narrow"),
    )
    ffn_summed = (
        lax.psum(grad_wleft.astype(jnp.bfloat16), "wide").astype(jnp.float32),
        lax.psum(grad_wright.astype(jnp.bfloat16), "wide").astype(jnp.float32),
        lax.psum(grad_wdown.astype(jnp.bfloat16), "wide").astype(jnp.float32),
    )
    grad_wq, grad_wk, grad_wv, grad_wg, grad_wo = (
        summed[0],
        summed[1],
        summed[2],
        summed[3],
        summed[4],
    )
    gain_one, gain_two = (summed[5], summed[6])
    sum_left, sum_right, sum_down = (ffn_summed[0], ffn_summed[1], ffn_summed[2])
    return (
        output[None],
        grad_tokens,
        grad_wq,
        grad_wk,
        grad_wv,
        grad_wg,
        grad_wo,
        gain_one,
        gain_two,
        sum_left,
        sum_right,
        sum_down,
    )


def solution(mesh):
    placed = (
        P("narrow", "wide", None),
        P("narrow", "wide", None),
        P("narrow", None),
        P(),
        P(),
        P(),
        P(),
        P(),
        P(),
        P(),
        P(),
        P(None, "narrow"),
        P(None, "narrow"),
        P("narrow", None),
    )
    return jax.shard_map(
        body,
        mesh=mesh,
        in_specs=placed,
        out_specs=(
            P("narrow", "wide", None),
            P("narrow", "wide", None),
            P(),
            P(),
            P(),
            P(),
            P(),
            P(),
            P(),
            P(None, "narrow"),
            P(None, "narrow"),
            P("narrow", None),
        ),
        check_vma=False,
    )
```

profile of v0, /device:TPU:0, one launch (start us, length us, event | category | flops | bytes accessed | tf_op | source)
XLA Modules:
  0.0 888.6 jit_solution(12251395130759058349)
XLA Ops:
  13.7 4.4 fusion.45
  18.1 2.8 multiply_convert_fusion.8
  25.7 3.5 fusion.46
  30.8 23.2 %all-reduce = bf16[64]{0:T(256)(128)(2,1)S(1)} all-reduce(bf16[64]{0:T(256)(128)(2,1)S(1)} %dynamic-update-slice), channel_id=2, replica_groups=mesh['wide'=8,'narrow'=4] {'wide'}, use_global_device_ids=true, to_apply=%add | all-reduce | flops 64 | bytes 256
  54.1 4.7 multiply_convert_fusion.9
  63.5 2.7 multiply_convert_fusion.1
  68.2 2.8 fusion.59
  71.0 10.6 %all-gather.11.cloned.1.call-done = bf16[64,128,128]{2,1,0:T(8,128)(2,1)} async-done(((bf16[8,128,128]{2,1,0:T(8,128)(2,1)}), bf16[64,128,128]{2,1,0:T(8,128)(2,1)}) %all-gather.11.cloned.1.call-update) | async-done | bytes 2097168 | tf_op jit(solution)/shard_map/all_gather | solution.py:15
  82.7 3.4 multiply_reduce_fusion.2
  88.1 2.9 copy.103
  90.9 4.4 multiply_convert_fusion.7
  100.2 46.5 %all-gather.9.cloned.1.call-done = bf16[2048,1024]{1,0:T(8,128)(2,1)} async-done(((bf16[512,1024]{1,0:T(8,128)(2,1)}), bf16[2048,1024]{1,0:T(8,128)(2,1)}) %all-gather.9.cloned.1.call-update) | async-done | bytes 4194320 | tf_op jit(solution)/shard_map/all_gather | solution.py:135
  146.7 8.5 fusion.99
  155.2 5.1 fusion.98
  160.3 22.5 %all-gather.13.cloned.1.call-done = bf16[1,2048,1024]{2,1,0:T(8,128)(2,1)} async-done(((bf16[1,512,1024]{2,1,0:T(8,128)(2,1)}), bf16[1,2048,1024]{2,1,0:T(8,128)(2,1)}) %all-gather.13.cloned.1.call-update) | async-done | bytes 4194320 | tf_op jit(solution)/shard_map/all_gather | solution.py:147
  182.8 11.0 %multiply_convert_fusion.2 = (bf16[2048,704]{0,1:T(8,128)(2,1)S(1)}, bf16[2048,704]{0,1:T(8,128)(2,1)}, bf16[2048,704]{0,1:T(8,128)(2,1)S(1)}) fusion(f32[2048,704]{0,1:T(8,128)} %fusion.98, f32[2048,704]{0,1:T(8,128)} %fusion.99, bf16[704,1024]{1,0:T(8,128)(2,1)} %param.31, bf16[1,2048,1024]{2,1,0:T(8,128)(2,1)} %all-gather.13.cloned.1.call-done), kind=kOutput, calls=%fused_computation.8 | convolution fusion | flops 2961440768 | bytes 25821184 | tf_op jit(solution)/shard_map/dot_general | solution.py:48
  193.8 3.5 fusion.100
  197.4 5.2 add_convert_fusion
  203.1 7.7 convolution_convert_fusion
  210.9 36.4 %reduce-scatter.5.cloned.1.call-done = bf16[512,1024]{1,0:T(8,128)(2,1)} async-done(((bf16[2048,1024]{1,0:T(8,128)(2,1)}), bf16[512,1024]{1,0:T(8,128)(2,1)}) %reduce-scatter.5.cloned.1.call-update) | async-done | bytes 1048592 | tf_op jit(solution)/shard_map/reduce_scatter | solution.py:154
  247.3 2.6 fusion.16
  249.9 45.0 %reduce-scatter.3.cloned.1.call-done = bf16[512,1024]{1,0:T(8,128)(2,1)} async-done(((bf16[2048,1024]{1,0:T(8,128)(2,1)}), bf16[512,1024]{1,0:T(8,128)(2,1)}) %reduce-scatter.3.cloned.1.call-update) | async-done | bytes 1048592 | tf_op jit(solution)/shard_map/reduce_scatter | solution.py:139
  295.0 4.3 fusion.21
  299.5 3.0 multiply_convert_fusion.5
  302.5 2.9 copy.104
  305.4 2.9 multiply_reduce_fusion
  312.6 7.5 fusion.42
  320.1 4.3 convolution_convert_fusion.1
  324.4 4.3 convolution_convert_fusion.2
  329.0 4.7 fusion.105
  333.7 2.7 multiply_convert_fusion
  340.8 2.9 copy.123
  343.7 4.8 fusion.84
  350.6 3.4 fusion.88
  356.4 3.3 fusion.77
  362.8 14.4 %while.27 = (s32[]{:T(128)}, f32[8,128,128]{2,1,0:T(8,128)}, s32[]{:T(128)}, bf16[8,8]{1,0:T(8,128)(2,1)S(1)}, bf16[8,8,128,128]{3,2,1,0:T(8,128)(2,1)}, /*index=5*/s32[]{:T(128)}, s32[]{:T(128)}, s32[]{:T(128)}, s32[]{:T(128)}) while((s32[]{:T(128)}, f32[8,128,128]{2,1,0:T(8,128)}, s32[]{:T(128)}, bf16[8,8]{1,0:T(8,128)(2,1)S(1)}, ...), condition=%wide.region_12.13_spmd, body=%wide.region_11.12_spmd.sunk | while | flops 393230 | bytes 1310955 | solution.py:30
  377.2 4.5 fusion.33
  381.7 3.1 copy.124
  384.8 3.2 fusion.32
  388.1 3.5 fusion.55
  393.6 3.4 fusion.86
  397.1 127.3 %all-reduce.9.cloned.1.call-done = (bf16[1024,704]{0,1:T(8,128)(2,1)}, bf16[1024,704]{0,1:T(8,128)(2,1)}, bf16[704,1024]{1,0:T(8,128)(2,1)}) async-done(((bf16[1024,704]{0,1:T(8,128)(2,1)}, bf16[1024,704]{0,1:T(8,128)(2,1)}, bf16[704,1024]{1,0:T(8,128)(2,1)}), (bf16[1024,704]{0,1:T(8,128)(2,1)}, bf16[1024,704]{0,1:T(8,128)(2,1)}, bf16[704,1024]{1,0:T(8,128)(2,1)})) %all-reduce.9.cloned.1.call-update) | async-done | bytes 4325392 | tf_op jit(solution)/shard_map/psum | solution.py:213
  524.4 3.4 convert_element_type.248
  538.5 3.1 fusion.14
  541.5 40.7 %all-reduce.1 = (f32[1024]{0:T(1024)}, f32[1024]{0:T(1024)}) all-reduce(f32[1024]{0:T(1024)S(1)} %get-tuple-element.144, f32[1024]{0:T(1024)S(1)} %get-tuple-element.142), channel_id=1, replica_groups=mesh['wide'=8,'narrow'=4] {'wide','narrow'}, use_global_device_ids=true, to_apply=%region_20.21 | all-reduce | flops 2048 | bytes 16384 | tf_op jit(solution)/shard_map/psum | solution.py:200
  582.2 4.1 fusion.30
  586.4 277.1 %all-reduce.7.cloned.1.call-done = (f32[1024,1024]{1,0:T(8,128)}, f32[1024,1024]{1,0:T(8,128)}, f32[1024,1024]{1,0:T(8,128)}, f32[1024,1024]{1,0:T(8,128)}, f32[1024,1024]{1,0:T(8,128)}) async-done(((f32[1024,1024]{1,0:T(8,128)}, f32[1024,1024]{1,0:T(8,128)}, f32[1024,1024]{1,0:T(8,128)}, f32[1024,1024]{1,0:T(8,128)}, f32[1024,1024]{1,0:T(8,128)}), (f32[1024,1024]{1,0:T(8,128)}, f32[1024,1024]{1,0:T(8,128)}, ...) | async-done | bytes 20971536 | tf_op jit(solution)/shard_map/psum | solution.py:200
  863.5 4.9 copy.174
  (218 shorter events, 82.8 us)
Async XLA Ops:
  7.2 83.8 %copy-start = (bf16[1024,1024]{1,0:T(8,128)(2,1)S(1)}, bf16[1024,1024]{1,0:T(8,128)(2,1)}, u32[]{:S(2)}) copy-start(bf16[1024,1024]{1,0:T(8,128)(2,1)} %param.26) | copy-start | bytes 6291460
  7.2 74.5 %all-gather.11.cloned.1.call-start = ((), (), s32[]{:S(2)}) async-start(), calls=%async_computation.5 | async-start | bytes 2359296 | tf_op jit(solution)/shard_map/all_gather | solution.py:15
  13.7 4.4 copy-start.1
  13.7 4.4 copy-start.47
  13.7 4.4 copy-start.61
  21.9 3.7 copy-start.57
  25.6 3.8 copy-start.67
  29.2 117.5 %all-gather.9.cloned.1.call-start = ((), (), s32[]{:S(2)}) async-start(), calls=%async_computation.2 | async-start | bytes 5242880 | tf_op jit(solution)/shard_map/all_gather | solution.py:135
  61.3 4.8 copy-start.50
  61.6 4.6 copy-start.48
  63.5 4.7 copy-start.37
  90.9 4.4 copy-start.43
  99.4 83.4 %all-gather.13.cloned.1.call-start = ((), (), s32[]{:S(2)}) async-start(), calls=%async_computation.6 | async-start | bytes 5242880 | tf_op jit(solution)/shard_map/all_gather | solution.py:147
  100.1 147.2 %reduce-scatter.5.cloned.1.call-start = ((), (), s32[]{:S(2)}) async-start(), calls=%async_computation.4 | async-start | bytes 5242880 | tf_op jit(solution)/shard_map/reduce_scatter | solution.py:154
  146.7 8.5 copy-start.58
  146.7 8.5 copy-start.64
  182.8 11.0 %copy-start.65 = (bf16[1024,704]{0,1:T(8,128)(2,1)S(1)}, bf16[1024,704]{0,1:T(8,128)(2,1)}, u32[]{:S(2)}) copy-start(bf16[1024,704]{0,1:T(8,128)(2,1)} %param.29) | copy-start | bytes 4325380
  193.8 3.5 copy-start.22
  193.8 3.5 copy-start.24
  193.8 3.5 copy-start.66
  202.6 92.4 %reduce-scatter.3.cloned.1.call-start = ((), (), s32[]{:S(2)}) async-start(), calls=%async_computation.3 | async-start | bytes 5242880 | tf_op jit(solution)/shard_map/reduce_scatter | solution.py:139
  210.8 151.1 %all-gather.15.cloned.1.call-start = ((), (), s32[]{:S(2)}) async-start(), calls=%async_computation.7 | async-start | bytes 2359296 | tf_op jit(solution)/shard_map/all_gather | solution.py:15
  295.0 4.3 copy-start.7
  295.0 4.3 copy-start.18
  295.0 4.5 copy-start.44
  305.4 3.5 copy-start.9
  312.5 211.9 %all-reduce.9.cloned.1.call-start = ((), (), s32[]{:S(2)}) async-start(), calls=%async_computation.9 | async-start | bytes 8650752 | tf_op jit(solution)/shard_map/psum | solution.py:213
  312.5 7.6 copy-start.25
  312.5 7.5 copy-start.59
  320.1 4.3 copy-start.23
  328.7 534.8 %all-reduce.7.cloned.1.call-start = ((), (), s32[]{:S(2)}) async-start(), calls=%async_computation.8 | async-start | bytes 41943040 | tf_op jit(solution)/shard_map/psum | solution.py:200
  328.9 4.8 copy-start.14
  328.9 4.7 copy-start.38
  328.9 4.7 copy-start.49
  328.9 4.7 copy-start.51
  343.7 4.8 copy-start.27
  343.7 4.8 copy-start.42
  350.6 3.4 copy-start.12
  350.6 3.4 copy-start.17
  388.1 3.5 copy-start.52
  388.1 3.5 copy-start.26
  388.1 3.5 copy-start.41
  524.4 3.4 copy-start.46
  538.5 43.8 %copy-start.56 = (f32[512]{0:T(512)S(1)}, f32[512]{0:T(512)}, u32[]{:S(2)}) copy-start(f32[512]{0:T(512)} %copy-done.55) | copy-start | bytes 6148
  863.5 4.9 copy-start.36
  868.4 3.7 copy-start.35
  872.1 3.7 copy-start.34
  875.9 3.7 copy-start.33
  (28 other events, 54.2 us)
Sparse Core Ops, SparseCore 0:
  29.3 52.2 all-gather.10
  99.5 47.1 all-gather.8
  148.3 34.4 all-gather.12
  202.7 44.5 reduce-scatter.4
  250.4 44.5 reduce-scatter.2
  312.6 49.2 all-gather.14
  365.8 158.4 all-reduce.8
  531.4 332.1 all-reduce.6
where the time goes:
time: 902 us; the launch traced here: 889 us
  waiting for transfers between devices  569 us (63%)
  matrix products  139 us (15%)
  blocking collectives  63.9 us (7%)
  local copies, waits for them, and re-layouts  54.5 us (6%)
  other arithmetic  45.1 us (5%)
  between operations  16.9 us (2%)
    psum x1, waiting for transfers between devices, body(): lax.psum((contract_rows(normed1, grad_qpre), contract_rows(normed1, grad_...  277 us
    psum x1, waiting for transfers between devices, body(): lax.psum(grad_wleft.astype(jnp.bfloat16), 'wide').astype(jnp.float32)  127 us
    all_gather x1, waiting for transfers between devices, body(): rows_all = lax.all_gather(normed2, 'narrow', axis=0, tiled=True)  46.5 us
    reduce_scatter x1, waiting for transfers between devices, body(): lax.psum_scatter(jnp.dot(product, w_down, preferred_element_type=f32).ast...  45 us
    psum x1, blocking collectives, body(): lax.psum((contract_rows(normed1, grad_qpre), contract_rows(normed1, grad_...  40.7 us
    reduce_scatter x1, waiting for transfers between devices, body(): lax.psum_scatter((times_transpose(grad_left, w_left) + times_transpose(gr...  36.4 us
    dot_general x8, matrix products, contract_rows(): lax.dot_general(left_mat, right_mat, (((0,), (0,)), ((), ())), preferred_...  34.5 us
    unnamed x145, local copies, waits for them, and re-layouts  34.3 us
  transfers between devices with their start and end apart: 8, of which 8 were waited for; matrix products, arithmetic and copies ran while one was open for 15% of the time, Pallas kernels for 0%

commit v1 on v0

--- a/solution.py
+++ b/solution.py
@@ -1,10 +1,782 @@
+import math
+
 import jax
 import jax.numpy as jnp
 from jax import lax
+from jax.experimental import pallas as pl
+from jax.experimental.pallas import tpu as pltpu
 from jax.sharding import PartitionSpec as P
 
 EPS = 1e-06
 HIGH = lax.Precision.HIGHEST
+
+MESH = pl.DeviceIdType.MESH
+F32 = jnp.float32
+BF16 = jnp.bfloat16
+VMEM_BYTES = 62 * 1024 * 1024
+ANY = pl.BlockSpec(memory_space=pl.ANY)
+IN_VMEM = pl.BlockSpec(memory_space=pltpu.VMEM)
+IN_SMEM = pl.BlockSpec(memory_space=pltpu.SMEM)
+
+
+class Refs:
+    def __init__(self, names, refs):
+        self.__dict__.update(zip(names, refs, strict=True))
+
+
+def call_kernel(body, name, number, ins, outs, scratch, cost):
+    names = list(ins) + list(outs) + list(scratch)
+
+    def kernel(*refs):
+        body(Refs(names, refs))
+
+    results = pl.pallas_call(
+        kernel,
+        name=name,
+        out_shape=list(outs.values()),
+        in_specs=[spec for _, spec in ins.values()],
+        out_specs=[ANY] * len(outs),
+        scratch_shapes=list(scratch.values()),
+        cost_estimate=pl.CostEstimate(flops=cost, bytes_accessed=cost // 500, transcendentals=0),
+        compiler_params=pltpu.CompilerParams(
+            collective_id=number, has_side_effects=True, vmem_limit_bytes=VMEM_BYTES
+        ),
+    )(*[array for array, _ in ins.values()])
+    return dict(zip(outs, results, strict=True))
+
+
+def nn(left, right):
+    return lax.dot_general(left, right, (((1,), (0,)), ((), ())), preferred_element_type=F32)
+
+
+def nt(left, right):
+    return lax.dot_general(left, right, (((1,), (1,)), ((), ())), preferred_element_type=F32)
+
+
+def tn(left, right):
+    return lax.dot_general(left, right, (((0,), (0,)), ((), ())), preferred_element_type=F32)
+
+
+def part(index, size):
+    return pl.ds(pl.multiple_of(index * size, size), size)
+
+
+def round_up(number, step):
+    return -(-number // step) * step
+
+
+class Place:
+    def __init__(self, wide):
+        self.wide = wide
+        self.lines = wide // 2
+        self.w = lax.axis_index("wide")
+        self.n = lax.axis_index("narrow")
+        self.core = lax.rem(self.n, 2)
+        self.xh = lax.div(self.n, 2)
+        self.yh = lax.rem(self.w, 2)
+        self.zi = lax.div(self.w, 2)
+        self.flip_core = (self.w, self.n + 1 - 2 * self.core)
+        self.flip_x = (self.w, self.n + 2 - 4 * self.xh)
+        self.flip_y = (self.w + 1 - 2 * self.yh, self.n)
+
+    def line(self, step):
+        return lax.rem(self.zi + step, self.lines)
+
+    def on_line(self, zi):
+        return (2 * zi + self.yh, self.n)
+
+    def on_wide(self, w):
+        return (w, self.n)
+
+
+def greet(partners, place, whole_wide):
+    barrier = pltpu.get_barrier_semaphore()
+    for partner in partners:
+        pl.semaphore_signal(barrier, inc=1, device_id=partner, device_id_type=MESH)
+    count = len(partners)
+    if whole_wide:
+
+        def one(step, carry):
+            pl.semaphore_signal(
+                barrier,
+                inc=1,
+                device_id=place.on_wide(lax.rem(place.w + step, place.wide)),
+                device_id_type=MESH,
+            )
+            return carry
+
+        lax.fori_loop(1, place.wide, one, 0)
+        count += place.wide - 1
+    pl.semaphore_wait(barrier, count)
+
+
+def remote(src, dst, send, recv, device):
+    return pltpu.make_async_remote_copy(
+        src_ref=src, dst_ref=dst, send_sem=send, recv_sem=recv, device_id=device, device_id_type=MESH
+    )
+
+
+def segment_ends(lens):
+    ends = []
+    total = jnp.int32(0)
+    for slot in range(lens.shape[1]):
+        total = total + lens[0, slot]
+        ends.append(total)
+    return ends
+
+
+def count_ends(ends, spots):
+    total = jnp.zeros_like(spots)
+    for end in ends:
+        total = total + jnp.where(spots >= end, 1, 0)
+    return total
+
+
+def segment_setup(place, ends, rate_row, rows, gate_ref, keep_ref, reach_ref):
+    anchor = place.w * rows
+    col_local = lax.broadcasted_iota(jnp.int32, (rows, 1), 0)
+    row_local = lax.broadcasted_iota(jnp.int32, (1, rows), 1)
+    col_seg = count_ends(ends, col_local + anchor)
+    row_seg = count_ends(ends, row_local + anchor)
+    before = jnp.int32(0)
+    last = jnp.int32(0)
+    for end in ends:
+        before = before + jnp.where(anchor - 1 >= end, 1, 0)
+        last = last + jnp.where(anchor + rows - 1 >= end, 1, 0)
+    before = jnp.where(place.w > 0, before, -1)
+    col_live = (col_local + anchor) < ends[-1]
+    row_live = (row_local + anchor) < ends[-1]
+    rates = rate_row[...]
+    steps = col_local.astype(F32)
+    gate_ref[...] = jnp.exp(-(steps + 1.0) * rates) * jnp.where(
+        (col_seg == before) & col_live, 1.0, 0.0
+    )
+    keep_ref[...] = jnp.exp(-(rows - 1.0 - steps) * rates) * jnp.where(
+        (col_seg == last) & col_live, 1.0, 0.0
+    )
+    gap = row_local - col_local
+    reaches = (gap >= 0) & (col_seg == row_seg) & row_live
+    reach_ref[...] = jnp.where(reaches, gap.astype(F32), -1.0)
+
+
+def decay_of(reach, rate):
+    return jnp.where(reach >= 0.0, jnp.exp(-rate * reach), 0.0)
+
+
+def scatter_states(place, local, arrived, sends, recvs, chunk):
+    def one(step, carry):
+        target = lax.rem(place.w + step, place.wide)
+        remote(
+            local.at[part(target, chunk)],
+            arrived.at[place.w],
+            sends.at[target],
+            recvs.at[place.w],
+            place.on_wide(target),
+        ).start()
+        return carry
+
+    lax.fori_loop(1, place.wide, one, 0)
+    arrived[place.w] = local[part(place.w, chunk), :]
+
+
+def wait_states(place, local, arrived, sends, recvs, chunk):
+    def one(step, carry):
+        source = lax.rem(place.w + step, place.wide)
+        copy = remote(
+            local.at[part(source, chunk)],
+            arrived.at[source],
+            sends.at[source],
+            recvs.at[source],
+            place.on_wide(source),
+        )
+        copy.wait_recv()
+        copy.wait_send()
+        return carry
+
+    lax.fori_loop(1, place.wide, one, 0)
+
+
+def join_states(place, ends, rate, rows, arrived, joined, backward):
+    shape = arrived.shape[1:]
+    fade = jnp.exp(jnp.full((1, shape[1]), -1.0 * rows, F32) * rate)
+
+    def one(step, state):
+        block = place.wide - 1 - step if backward else step
+        joined[block] = state.astype(BF16)
+        cuts = jnp.int32(0)
+        for end in ends:
+            inside = (end >= block * rows) & (end <= block * rows + rows - 1)
+            cuts = cuts + jnp.where(inside, 1, 0)
+        flag = jnp.where((cuts == 0) & (block > 0), 1.0, 0.0)
+        return (fade * flag) * state + arrived[block].astype(F32)
+
+    lax.fori_loop(0, place.wide, one, jnp.zeros(shape, F32))
+
+
+def return_states(place, joined, entering, sends, recvs, chunk):
+    def one(step, carry):
+        target = lax.rem(place.w + step, place.wide)
+        remote(
+            joined.at[target],
+            entering.at[part(place.w, chunk)],
+            sends.at[target],
+            recvs.at[place.w],
+            place.on_wide(target),
+        ).start()
+        return carry
+
+    lax.fori_loop(1, place.wide, one, 0)
+    entering[part(place.w, chunk), :] = joined[place.w]
+
+
+def wait_returned(place, joined, entering, sends, recvs, chunk):
+    def one(step, carry):
+        source = lax.rem(place.w + step, place.wide)
+        copy = remote(
+            joined.at[source],
+            entering.at[part(source, chunk)],
+            sends.at[source],
+            recvs.at[source],
+            place.on_wide(source),
+        )
+        copy.wait_recv()
+        copy.wait_send()
+        return carry
+
+    lax.fori_loop(1, place.wide, one, 0)
+
+
+class Unit:
+    def __init__(self, place, kind, acc, other, xrecv, yrecv, zrecv, out, sems, zsems, index):
+        self.place = place
+        self.kind = kind
+        self.acc = acc
+        self.other = other
+        self.xrecv = xrecv
+        self.yrecv = yrecv
+        self.zrecv = zrecv
+        self.out = out
+        self.sems = sems.at[index]
+        self.zsems = zsems.at[index]
+        p = place
+        rows = out.shape[0]
+        if kind == "attn":
+            cols = part(p.core, out.shape[1] // 2)
+            self.half = rows // 2
+            self.quarter = rows // 4
+            self.chunk = self.quarter // p.lines
+            self.x_region = out.at[part(p.xh, self.half), cols]
+            self.core_region = out.at[:, cols]
+            y_base = p.xh * self.half + p.yh * self.quarter
+            self.y_region = out.at[pl.ds(pl.multiple_of(y_base, self.quarter), self.quarter), cols]
+            self.z_base, self.z_cols = y_base, cols
+            self.acc_base = y_base
+        elif kind == "rows":
+            self.half = rows // 2
+            self.chunk = self.half // p.lines
+            self.y_region = out.at[part(p.yh, self.half), :]
+            self.z_base, self.z_cols = p.yh * self.half, slice(None)
+            self.acc_base = 0
+        else:
+            cols = part(p.yh, out.shape[1] // 2)
+            self.chunk = rows // p.lines
+            self.y_region = out.at[:, cols]
+            self.z_base, self.z_cols = 0, cols
+            self.acc_base = 0
+
+    def pair(self, step, src, dst, device):
+        return remote(src, dst, self.sems.at[2 * step], self.sems.at[2 * step + 1], device)
+
+    def own_rows(self, base, zi):
+        start = pl.multiple_of(base + zi * self.chunk, self.chunk)
+        return pl.ds(start, self.chunk)
+
+    def x_copy(self):
+        src = self.acc.at[part(1 - self.place.xh, self.half)]
+        return self.pair(0, src, self.xrecv, self.place.flip_x)
+
+    def x_start(self):
+        self.x_copy().start()
+
+    def x_finish(self):
+        copy = self.x_copy()
+        copy.wait_recv()
+        base = self.place.xh * self.half
+        add_into(self.acc, base, self.xrecv)
+        self.y_start()
+
+    def y_copy(self):
+        if self.kind == "attn":
+            base = self.place.xh * self.half + (1 - self.place.yh) * self.quarter
+            src = self.acc.at[pl.ds(pl.multiple_of(base, self.quarter), self.quarter)]
+        else:
+            src = self.other
+        return self.pair(1, src, self.yrecv, self.place.flip_y)
+
+    def y_start(self):
+        self.y_copy().start()
+
+    def y_finish(self):
+        self.y_copy().wait_recv()
+        add_into(self.acc, self.acc_base, self.yrecv)
+        for step in range(1, self.place.lines):
+            self.z_copy(step).start()
+
+    def z_copy(self, step):
+        zi = self.place.line(step)
+        return remote(
+            self.acc.at[self.own_rows(self.acc_base, zi)],
+            self.zrecv.at[step - 1],
+            self.zsems.at[0, step],
+            self.zsems.at[1, step],
+            self.place.on_line(zi),
+        )
+
+    def z_finish(self):
+        for step in range(1, self.place.lines):
+            self.z_copy(step).wait_recv()
+        mine = self.own_rows(self.acc_base, self.place.zi)
+        total = self.acc[mine, :].astype(F32)
+        for step in range(1, self.place.lines):
+            total = total + self.zrecv[step - 1].astype(F32)
+        self.acc[mine, :] = total.astype(BF16)
+        self.local_copy().start()
+        for step in range(1, self.place.lines):
+            self.back_copy(step).start()
+
+    def local_copy(self):
+        return pltpu.make_async_copy(
+            self.acc.at[self.own_rows(self.acc_base, self.place.zi)],
+            self.out.at[self.own_rows(self.z_base, self.place.zi), self.z_cols],
+            self.zsems.at[2, 0],
+        )
+
+    def back_copy(self, step):
+        return remote(
+            self.acc.at[self.own_rows(self.acc_base, self.place.zi)],
+            self.out.at[self.own_rows(self.z_base, self.place.zi), self.z_cols],
+            self.zsems.at[2, step],
+            self.zsems.at[3, step],
+            self.place.on_line(self.place.line(step)),
+        )
+
+    def back_y_copy(self):
+        return self.pair(2, self.y_region, self.y_region, self.place.flip_y)
+
+    def back_z_finish(self):
+        self.local_copy().wait()
+        for step in range(1, self.place.lines):
+            self.back_copy(step).wait_recv()
+        self.back_y_copy().start()
+
+    def back_x_copy(self):
+        return self.pair(3, self.x_region, self.x_region, self.place.flip_x)
+
+    def back_y_finish(self):
+        self.back_y_copy().wait_recv()
+        if self.kind == "attn":
+            self.back_x_copy().start()
+
+    def back_core_copy(self):
+        return self.pair(4, self.core_region, self.core_region, self.place.flip_core)
+
+    def back_x_finish(self):
+        self.back_x_copy().wait_recv()
+        self.back_core_copy().start()
+
+    def close(self):
+        if self.kind == "attn":
+            self.back_core_copy().wait_recv()
+            self.x_copy().wait_send()
+            self.back_x_copy().wait_send()
+            self.back_core_copy().wait_send()
+        self.y_copy().wait_send()
+        self.back_y_copy().wait_send()
+        for step in range(1, self.place.lines):
+            self.z_copy(step).wait_send()
+            self.back_copy(step).wait_send()
+
+
+def add_into(acc, base, other):
+    rows = other.shape[0]
+    tile = math.gcd(rows, 128)
+
+    @pl.loop(0, rows // tile)
+    def _(i):
+        here = pl.ds(pl.multiple_of(base + i * tile, tile), tile)
+        acc[here, :] = acc[here, :] + other[part(i, tile), :]
+
+
+def backward_body(wide, heads, eps, r):
+    p = Place(wide)
+    lines = p.lines
+    rows, width = r.gn2.shape
+    head = width // heads
+    half = width // 2
+    tile = 128
+    chunk = width // wide
+    mine = part(p.core, half)
+    theirs = part(1 - p.core, half)
+
+    greet([p.flip_core, p.flip_x], p, True)
+
+    names = ("d", "l", "r", "o", "g", "q", "k", "v")
+    u = {}
+    for i, nm in enumerate(names):
+        if nm in "lr":
+            src = getattr(r, "p_" + nm).at[part(1 - p.yh, width // 2), :]
+            u[nm] = Unit(p, "rows", getattr(r, "acc_" + nm), src, None, getattr(r, "yr_" + nm), getattr(r, "zr_" + nm), getattr(r, "out_" + nm), r.usem, r.zsem, i)
+        elif nm == "d":
+            src = r.p_d.at[:, part(1 - p.yh, width // 2)]
+            u[nm] = Unit(p, "cols", r.acc_d, src, None, r.yr_d, r.zr_d, r.out_d, r.usem, r.zsem, i)
+        else:
+            k = i - 3
+            u[nm] = Unit(p, "attn", r.acc.at[k], None, r.xr.at[k], r.yr.at[k], r.zr.at[k], getattr(r, "out_" + nm), r.usem, r.zsem, i)
+
+    loads = {}
+
+    def load(key, src, dst):
+        loads[key] = pltpu.make_async_copy(src, dst, r.lsem.at[len(loads)])
+        loads[key].start()
+
+    def need(*keys):
+        for key in keys:
+            loads[key].wait()
+
+    load("gn2", r.gn2, r.gn2_v)
+    load("hidden", r.hidden, r.hid_v)
+    load("cot", r.cot, r.cot_v)
+    load("wo", r.wo, r.wa)
+    load("flat", r.flat, r.flat_v)
+    load("gate", r.gate, r.gate_v)
+    load("ko", r.ko, r.ko_v)
+    load("q", r.q, r.q_v)
+    for nm in "dlr":
+        u[nm].y_start()
+    to_sib = [
+        remote(r.mixed, r.mix_v.at[1], r.csem.at[0], r.csem.at[1], p.flip_core),
+        remote(r.n1, r.n1_v.at[1], r.csem.at[2], r.csem.at[3], p.flip_core),
+    ]
+    for copy in to_sib:
+        copy.start()
+    load("mixed", r.mixed, r.mix_v.at[0])
+    load("n1", r.n1, r.n1_v.at[0])
+    load("k", r.k, r.k_v)
+    load("v", r.v, r.v_v)
+    load("sin", r.sin, r.sin_v)
+    load("dq", r.dq, r.dq_v)
+    load("dk", r.dk, r.dk_v)
+    load("accd", r.p_d.at[:, part(p.yh, width // 2)], r.acc_d.at[pl.ds(0, r.p_d.shape[0])])
+    load("accl", r.p_l.at[part(p.yh, width // 2), :], r.acc_l)
+    load("accr", r.p_r.at[part(p.yh, width // 2), :], r.acc_r)
+    load("wk", r.wk, r.wc)
+    load("wv", r.wv, r.wd)
+
+    ends = segment_ends(r.lens)
+    segment_setup(p, ends, r.rate_row, rows, r.gate_in, r.keep_out, r.reach)
+
+    need("gn2", "hidden", "cot")
+    r.gsum[...] = jnp.zeros_like(r.gsum)
+
+    def fold(x):
+        return jnp.sum(x.reshape(x.shape[0] // 8, 8, x.shape[1]), axis=0)
+
+    @pl.loop(0, rows // tile)
+    def _(i):
+        here = part(i, tile)
+        hid = r.hid_v[here, :]
+        scale = lax.rsqrt(jnp.mean(hid * hid, axis=-1, keepdims=True) + eps)
+        unit = hid * scale
+        up = r.gn2_v[here, :]
+        r.gsum[1] += fold(up * unit)
+        up = up * r.fgain[...]
+        down = scale * (up - unit * jnp.mean(up * unit, axis=-1, keepdims=True))
+        down = down + r.cot_v[here, :].astype(F32)
+        r.hid_v[here, :] = down
+        r.gb[here, :] = down.astype(BF16)
+
+    load("tok", r.tokens, r.cot_v)
+    halves = {}
+
+    def send_half(key, src, slot):
+        halves[key] = remote(src.at[:, theirs], r.sib.at[slot], r.csem.at[4 + 2 * slot], r.csem.at[5 + 2 * slot], p.flip_core)
+        halves[key].start()
+
+    send_half("o", r.gb, 0)
+
+    need("wo", "flat", "gate", "ko")
+
+    @pl.loop(0, rows // 256)
+    def _(i):
+        here = part(i, 256)
+        gm = nt(r.gb[here, :], r.wa[...])
+        flat = r.flat_v[here, :].astype(F32)
+        r.gg[here, :] = (gm * flat).astype(BF16)
+        gm = gm * r.gate_v[here, :].astype(F32)
+        ko = r.ko_v[here, :]
+        for h in range(heads):
+            cols = slice(h * head, (h + 1) * head)
+            up, unit = gm[:, cols], flat[:, cols]
+            mean = jnp.mean(up * unit, axis=-1, keepdims=True)
+            r.ga[here, cols] = (ko[:, h : h + 1] * (up - unit * mean)).astype(BF16)
+
+    send_half("g", r.gg, 1)
+    load("wq", r.wq, r.wa)
+
+    need("q")
+    for h in range(heads):
+        cols = slice(h * head, (h + 1) * head)
+        gated = (r.q_v[:, cols].astype(F32) * r.gate_in[:, h : h + 1]).astype(BF16)
+        r.state_a[pl.ds(h * head, head), :] = tn(gated, r.ga[:, cols]).astype(BF16)
+    scatter_states(p, r.state_a, r.arrived, r.ssem.at[0], r.ssem.at[1], chunk)
+
+    def weight_unit(nm, slot, left, own):
+        acc = r.acc.at["ogqkv".index(nm)]
+        other = r.sib.at[slot]
+        halves[nm].wait_recv()
+
+        @pl.loop(0, width // 512)
+        def _(i):
+            here = part(i, 512)
+            acc[here, :] = (
+                tn(left[0, :, here], own[:, mine]) + tn(left[1, :, here], other[...])
+            ).astype(BF16)
+
+        u[nm].x_start()
+
+    need("mixed", "n1")
+    for copy in to_sib:
+        copy.wait_recv()
+    weight_unit("o", 0, r.mix_v, r.gb)
+    weight_unit("g", 1, r.n1_v, r.gg)
+
+    need("k", "v", "sin", "dq", "dk")
+
+    def inside(h, carry):
+        cols = part(h, head)
+        q, k, v, ga = r.q_v[:, cols], r.k_v[:, cols], r.v_v[:, cols], r.ga[:, cols]
+        weight = decay_of(r.reach[...], r.rate_s[h])
+        probs = (nt(k, q) * weight).astype(BF16)
+        r.gv_f[:, cols] = nn(probs, ga)
+        scores = (nt(v, ga) * weight).astype(BF16)
+        r.gn2_v[:, cols] = nn(scores, q)
+        pick = lax.broadcasted_iota(jnp.int32, (1, heads), 1) == h
+        gate = jnp.sum(jnp.where(pick, r.gate_in[...], 0.0), axis=1, keepdims=True)
+        gq = tn(scores, k) + nt(ga, r.sin_v[cols, :]) * gate
+        r.gq[:, cols] = (gq * r.dq_v[:, cols].astype(F32)).astype(BF16)
+        return carry
+
+    lax.fori_loop(0, heads // 2, inside, 0)
+    need("accd", "accl", "accr")
+    u["d"].y_finish()
+    wait_states(p, r.state_a, r.arrived, r.ssem.at[0], r.ssem.at[1], chunk)
+    join_states(p, ends, r.rate_s[lax.div(p.w * chunk, head)], rows, r.arrived, r.joined, True)
+    return_states(p, r.joined, r.state_b, r.ssem.at[2], r.ssem.at[3], chunk)
+    u["o"].x_finish()
+    lax.fori_loop(heads // 2, heads, inside, 0)
+    send_half("q", r.gq, 2)
+    u["g"].x_finish()
+    u["l"].y_finish()
+    weight_unit("q", 2, r.n1_v, r.gq)
+    wait_returned(p, r.joined, r.state_b, r.ssem.at[2], r.ssem.at[3], chunk)
+
+    for h in range(heads):
+        cols = slice(h * head, (h + 1) * head)
+        state = r.state_b[pl.ds(h * head, head), :]
+        keep = r.keep_out[:, h : h + 1]
+        gk = r.gn2_v[:, cols] + nt(r.v_v[:, cols], state) * keep
+        r.flat_v[:, cols] = (gk * r.dk_v[:, cols].astype(F32)).astype(BF16)
+        gv = r.gv_f[:, cols] + nn(r.k_v[:, cols], state) * keep
+        r.gate_v[:, cols] = gv.astype(BF16)
+    send_half("k", r.flat_v, 3)
+    send_half("v", r.gate_v, 4)
+    weight_unit("k", 3, r.n1_v, r.flat_v)
+    weight_unit("v", 4, r.n1_v, r.gate_v)
+    to_sib[0].wait_send()
+    load("wg0", r.wg.at[pl.ds(0, rows)], r.mix_v.at[0])
+    load("wg1", r.wg.at[pl.ds(rows, rows)], r.mix_v.at[1])
+    u["d"].z_finish()
+    u["r"].y_finish()
+    u["o"].y_finish()
+    u["g"].y_finish()
+
+    need("wq", "wk", "wv", "wg0", "wg1", "tok")
+
+    @pl.loop(0, rows // tile)
+    def _(i):
+        here = part(i, tile)
+        up = (
+            nt(r.gq[here, :], r.wa[...])
+            + nt(r.flat_v[here, :], r.wc[...])
+            + nt(r.gate_v[here, :], r.wd[...])
+            + jnp.concatenate([nt(r.gg[here, :], r.mix_v[i]) for i in range(2)], axis=1)
+        )
+        tok = r.cot_v[here, :].astype(F32)
+        scale = lax.rsqrt(jnp.mean(tok * tok, axis=-1, keepdims=True) + eps)
+        unit = tok * scale
+        r.gsum[0] += fold(up * unit)
+        up = up * r.again[...]
+        down = scale * (up - unit * jnp.mean(up * unit, axis=-1, keepdims=True))
+        r.hid_v[here, :] += down
+
+    store = pltpu.make_async_copy(r.hid_v, r.gtok, r.osem.at[0])
+    store.start()
+
+    r.gains[0] = jnp.zeros_like(r.gains[0])
+    for row in range(2):
+        r.gains[0, pl.ds(row, 1), :] = jnp.sum(r.gsum[row], axis=0, keepdims=True)
+
+    def gain_copy(step, device):
+        return remote(r.gains.at[step], r.grecv.at[step], r.gsem.at[2 * step], r.gsem.at[2 * step + 1], device)
+
+    def gain_line(step):
+        return remote(
+            r.gains.at[3],
+            r.grecv.at[3 + p.zi],
+            r.gsem.at[6 + 2 * step],
+            r.gsem.at[7 + 2 * step],
+            p.on_line(p.line(step)),
+        )
+
+    def gain_next(step, device):
+        copy = gain_copy(step, device)
+        copy.wait_recv()
+        r.gains[step + 1] = r.gains[step] + r.grecv[step]
+
+    gain_copy(0, p.flip_core).start()
+    u["l"].z_finish()
+    u["q"].x_finish()
+    gain_next(0, p.flip_core)
+    gain_copy(1, p.flip_x).start()
+    u["k"].x_finish()
+    u["q"].y_finish()
+    u["o"].z_finish()
+    u["g"].z_finish()
+    gain_next(1, p.flip_x)
+    gain_copy(2, p.flip_y).start()
+    u["d"].back_z_finish()
+    u["v"].x_finish()
+    u["r"].z_finish()
+    u["k"].y_finish()
+    u["q"].z_finish()
+    gain_next(2, p.flip_y)
+    for step in range(1, lines):
+        gain_line(step).start()
+    u["v"].y_finish()
+    u["k"].z_finish()
+    u["o"].back_z_finish()
+    u["g"].back_z_finish()
+    u["l"].back_z_finish()
+    u["v"].z_finish()
+    u["o"].back_y_finish()
+    u["g"].back_y_finish()
+    u["q"].back_z_finish()
+    u["k"].back_z_finish()
+    u["v"].back_z_finish()
+    u["r"].back_z_finish()
+    for nm in "qkv":
+        u[nm].back_y_finish()
+    for nm in "ogqkv":
+        u[nm].back_x_finish()
+    for nm in "dlr":
+        u[nm].back_y_finish()
+    for step in range(1, lines):
+        gain_line(step).wait_recv()
+    r.grecv[3 + p.zi] = r.gains[3]
+    total = r.grecv[3]
+    for zi in range(1, lines):
+        total = total + r.grecv[3 + zi]
+    r.gains[4] = total
+    put = pltpu.make_async_copy(r.gains.at[4], r.out_gain, r.osem.at[1])
+    put.start()
+    for nm in names:
+        u[nm].close()
+    put.wait()
+    store.wait()
+    to_sib[1].wait_send()
+    for copy in halves.values():
+        copy.wait_send()
+    for step, device in enumerate((p.flip_core, p.flip_x, p.flip_y)):
+        gain_copy(step, device).wait_send()
+    for step in range(1, lines):
+        gain_line(step).wait_send()
+
+
+def backward_call(wide, heads, eps, arrays):
+    rows, width = arrays["gn2"].shape
+    hidden = arrays["p_l"].shape[1]
+    lines = wide // 2
+    half, quarter = width // 2, width // 4
+    tall = lines * round_up(-(-hidden // lines), 16)
+    specs = {"lens": IN_SMEM, "rate_s": IN_SMEM, "rate_row": IN_VMEM, "fgain": IN_VMEM, "again": IN_VMEM}
+    ins = {nm: (a, specs.get(nm, ANY)) for nm, a in arrays.items()}
+    sds = jax.ShapeDtypeStruct
+    outs = {"out_" + nm: sds((width, width), BF16) for nm in "ogqkv"}
+    outs["out_l"] = sds((width, hidden), BF16)
+    outs["out_r"] = sds((width, hidden), BF16)
+    outs["out_d"] = sds((tall, width), BF16)
+    outs["gtok"] = sds((rows, width), F32)
+    outs["out_gain"] = sds((8, width), F32)
+    V = pltpu.VMEM
+    dma = pltpu.SemaphoreType.DMA
+    scratch = dict(
+        gn2_v=V((rows, width), F32),
+        hid_v=V((rows, width), F32),
+        gv_f=V((rows, width), F32),
+        cot_v=V((rows, width), BF16),
+        flat_v=V((rows, width), BF16),
+        gate_v=V((rows, width), BF16),
+        ko_v=V((rows, heads), F32),
+        q_v=V((rows, width), BF16),
+        k_v=V((rows, width), BF16),
+        v_v=V((rows, width), BF16),
+        dq_v=V((rows, width), BF16),
+        dk_v=V((rows, width), BF16),
+        mix_v=V((2, rows, width), BF16),
+        n1_v=V((2, rows, width), BF16),
+        sin_v=V((width, width // heads), BF16),
+        wa=V((width, width), BF16),
+        wc=V((width, width), BF16),
+        wd=V((width, width), BF16),
+        gb=V((rows, width), BF16),
+        gg=V((rows, width), BF16),
+        ga=V((rows, width), BF16),
+        gq=V((rows, width), BF16),
+        sib=V((5, rows, half), BF16),
+        gate_in=V((rows, heads), F32),
+        keep_out=V((rows, heads), F32),
+        reach=V((rows, rows), F32),
+        state_a=V((width, width // heads), BF16),
+        state_b=V((width, width // heads), BF16),
+        arrived=V((wide, width // wide, width // heads), BF16),
+        joined=V((wide, width // wide, width // heads), BF16),
+        acc=V((5, width, half), BF16),
+        xr=V((5, half, half), BF16),
+        yr=V((5, quarter, half), BF16),
+        zr=V((5, lines - 1, quarter // lines, half), BF16),
+        acc_d=V((tall, half), BF16),
+        acc_l=V((half, hidden), BF16),
+        acc_r=V((half, hidden), BF16),
+        yr_d=V((hidden, half), BF16),
+        yr_l=V((half, hidden), BF16),
+        yr_r=V((half, hidden), BF16),
+        zr_d=V((lines - 1, tall // lines, half), BF16),
+        zr_l=V((lines - 1, half // lines, hidden), BF16),
+        zr_r=V((lines - 1, half // lines, hidden), BF16),
+        gsum=V((2, 8, width), F32),
+        gains=V((5, 8, width), F32),
+        grecv=V((3 + lines, 8, width), F32),
+        lsem=dma((24,)),
+        csem=dma((14,)),
+        ssem=dma((4, wide)),
+        usem=dma((8, 10)),
+        zsem=dma((8, 4, lines)),
+        gsem=dma((8 + 2 * lines,)),
+        osem=dma((2,)),
+    )
+    return call_kernel(
+        lambda r: backward_body(wide, heads, eps, r), "attention_backward", 3, ins, outs, scratch, 20 * 10**9
+    )
 
 
 def carried_in(array, axis, join, neutral, backward):
@@ -159,83 +931,57 @@
         scatter_dimension=0,
         tiled=True,
     ).astype(jnp.float32)
-    grad_hid_part, grad_gain_two = norm_back2(grad_normed2)
-    grad_hidden = grad_out.astype(f32) + grad_hid_part
-    grad_branch = grad_hidden.astype(bf16)
-    grad_mixed = times_transpose(grad_branch, w_out)
-    grad_gate = (grad_mixed * flat_o).astype(bf16)
-    grad_flat = (grad_mixed * gate_u).reshape(head_shape)
-    grad_attn = head_back(grad_flat)[0].astype(bf16)
-    grad_attn_wide = grad_attn.astype(f32)
-    grad_probs = jnp.einsum("thd,shd->hts", grad_attn, value, preferred_element_type=f32)
-    grad_scores = (grad_probs * decay_mask).astype(bf16)
-    local_back = jnp.einsum(
-        "thd,the->hde", query_wide * gate_in.T[:, :, None], grad_attn_wide, precision=HIGH
-    )
-    state_out = carried_in((pass_on, local_back), "wide", combine_affine, identity, True)[1]
-    grad_query = (
-        jnp.einsum("hts,shd->thd", grad_scores, keyed, preferred_element_type=f32)
-        + jnp.einsum("the,hde->thd", grad_attn_wide, state_in, precision=HIGH)
-        * gate_in.T[:, :, None]
-    )
-    grad_key = (
-        jnp.einsum("hts,thd->shd", grad_scores, query, preferred_element_type=f32)
-        + jnp.einsum("hde,she->shd", state_out, value_wide, precision=HIGH) * keep_out.T[:, :, None]
-    )
-    grad_value = (
-        jnp.einsum("hts,thd->shd", probs, grad_attn, preferred_element_type=f32)
-        + jnp.einsum("hde,shd->she", state_out, keyed_wide, precision=HIGH) * keep_out.T[:, :, None]
-    )
-    grad_qpre = query_back(grad_query.reshape(rows_dev, model_width))[0].astype(bf16)
-    grad_kpre = key_back(grad_key.reshape(rows_dev, model_width))[0].astype(bf16)
-    grad_vpre = grad_value.reshape(rows_dev, model_width).astype(bf16)
-    grad_normed1 = (
-        times_transpose(grad_qpre, w_query)
-        + times_transpose(grad_kpre, w_key)
-        + times_transpose(grad_vpre, w_value)
-        + times_transpose(grad_gate, w_gate)
-    )
-    grad_in_part, grad_gain_one = norm_back1(grad_normed1)
-    grad_tokens = (grad_hidden + grad_in_part)[None]
-    summed = lax.psum(
-        (
-            contract_rows(normed1, grad_qpre),
-            contract_rows(normed1, grad_kpre),
-            contract_rows(normed1, grad_vpre),
-            contract_rows(normed1, grad_gate),
-            contract_rows(mixed, grad_branch),
-            grad_gain_one,
-            grad_gain_two,
+    rows_flat = lambda a: a.reshape(rows_dev, model_width)
+    slope = lambda x: jax.nn.sigmoid(x) * (1.0 + x * (1.0 - jax.nn.sigmoid(x)))
+    done = backward_call(
+        lax.axis_size("wide"),
+        num_heads,
+        EPS,
+        dict(
+            gn2=grad_normed2,
+            hidden=hidden,
+            cot=grad_out,
+            wo=w_out,
+            flat=flat_o.astype(bf16),
+            gate=gate_u.astype(bf16),
+            ko=lax.rsqrt(jnp.mean(attn_raw * attn_raw, axis=-1) + EPS),
+            q=rows_flat(query),
+            k=rows_flat(keyed),
+            v=rows_flat(value),
+            mixed=mixed,
+            n1=normed1,
+            sin=state_in.reshape(model_width, head_dim).astype(bf16),
+            dq=slope(q_pre).astype(bf16),
+            dk=slope(k_pre).astype(bf16),
+            p_d=grad_wdown.astype(bf16),
+            p_l=grad_wleft.astype(bf16),
+            p_r=grad_wright.astype(bf16),
+            wq=w_query,
+            wk=w_key,
+            wv=w_value,
+            wg=w_gate,
+            tokens=tokens[0],
+            lens=lengths,
+            rate_s=decay_rate,
+            rate_row=decay_rate[None],
+            fgain=ffn_gain[None],
+            again=attn_gain[None],
         ),
-        ("wide", "narrow"),
-    )
-    ffn_summed = (
-        lax.psum(grad_wleft.astype(jnp.bfloat16), "wide").astype(jnp.float32),
-        lax.psum(grad_wright.astype(jnp.bfloat16), "wide").astype(jnp.float32),
-        lax.psum(grad_wdown.astype(jnp.bfloat16), "wide").astype(jnp.float32),
-    )
-    grad_wq, grad_wk, grad_wv, grad_wg, grad_wo = (
-        summed[0],
-        summed[1],
-        summed[2],
-        summed[3],
-        summed[4],
-    )
-    gain_one, gain_two = (summed[5], summed[6])
-    sum_left, sum_right, sum_down = (ffn_summed[0], ffn_summed[1], ffn_summed[2])
+    )
+    wide_of = lambda nm: done["out_" + nm].astype(f32)
     return (
         output[None],
-        grad_tokens,
-        grad_wq,
-        grad_wk,
-        grad_wv,
-        grad_wg,
-        grad_wo,
-        gain_one,
-        gain_two,
-        sum_left,
-        sum_right,
-        sum_down,
+        done["gtok"][None],
+        wide_of("q"),
+        wide_of("k"),
+        wide_of("v"),
+        wide_of("g"),
+        wide_of("o"),
+        done["out_gain"][0],
+        done["out_gain"][1],
+        wide_of("l"),
+        wide_of("r"),
+        wide_of("d")[: w_down.shape[0]],
     )
 
 

time: 902 us -> 549 us (0.61); the launches traced: 889 us -> 546 us
  waiting for transfers between devices: 569 us -> 88.9 us
  Pallas kernels: 0 us -> 263 us
  matrix products: 139 us -> 89.7 us
  blocking collectives: 63.9 us -> 23.2 us
  local copies, waits for them, and re-layouts: 54.5 us -> 22.4 us
  other arithmetic: 45.1 us -> 31.3 us
  loops' own time: 0.16 us -> 10.7 us
    psum x2 -> x0, waiting for transfers between devices: 404 us -> none  [the longest x1 277 us: body(): lax.psum((contract_rows(normed1, grad_qpre), contract_rows(normed1, grad_...]
    pallas_call x0 -> x1, Pallas kernels: none -> 263 us  [call_kernel(): pl.pallas_call(kernel, name=name, out_shape=list(outs.values()), in_specs...]
    reduce_scatter x1, waiting for transfers between devices: 45 us -> 0.01 us  [body(): lax.psum_scatter(jnp.dot(product, w_down, preferred_element_type=f32).ast...]
    psum x1 -> x0, blocking collectives: 40.7 us -> none  [body(): lax.psum((contract_rows(normed1, grad_qpre), contract_rows(normed1, grad_...]
    dot_general x9 -> x0, matrix products: 25.7 us -> none  [the longest x1 4.71 us: body(): jnp.einsum('hts,thd->shd', probs, grad_attn, preferred_element_type=f32)]
    reduce_scatter x1, waiting for transfers between devices: 36.4 us -> 11.6 us  [body(): lax.psum_scatter((times_transpose(grad_left, w_left) + times_transpose(gr...]
    unnamed x145 -> x60, local copies, waits for them, and re-layouts: 34.3 us -> 9.83 us
    add x8 -> x0, other arithmetic: 18.7 us -> none  [the longest x7 14.4 us: combine_affine(): later[0][:, None, None] * earlier[1] + later[1]]
  transfers between devices with their start and end apart: 8 -> 5, of which waited for: 8 -> 4; matrix products, arithmetic and copies ran while one was open for 15% -> 16% of each run, Pallas kernels for 0% -> 48%
where the time goes in v1:
time: 549 us; the launch traced here: 546 us
  Pallas kernels  263 us (48%)
  matrix products  89.7 us (16%)
  waiting for transfers between devices  88.9 us (16%)
  other arithmetic  31.3 us (6%)
  blocking collectives  23.2 us (4%)
  local copies, waits for them, and re-layouts  22.4 us (4%)
  between operations  16.3 us (3%)
  loops' own time  10.7 us (2%)
    pallas_call x1, Pallas kernels, call_kernel(): pl.pallas_call(kernel, name=name, out_shape=list(outs.values()), in_specs...  263 us
    all_gather x1, waiting for transfers between devices, body(): rows_all = lax.all_gather(normed2, 'narrow', axis=0, tiled=True)  40.4 us
    unnamed x1, blocking collectives  23.2 us
    all_gather x1, waiting for transfers between devices, body(): grad_all = lax.all_gather(grad_out, 'narrow', axis=0, tiled=True)  21.1 us
    dot_general x3, matrix products, contract_rows(): lax.dot_general(left_mat, right_mat, (((0,), (0,)), ((), ())), preferred_...  20.9 us
    dot_general x3, matrix products, times_transpose(): lax.dot_general(left_mat, right_mat, (((1,), (1,)), ((), ())), preferred_...  17.4 us
    all_gather x1, waiting for transfers between devices, carried_in(): lax.all_gather(a.astype(kind), axis)  14.9 us
    convert_element_type x6, other arithmetic, body(): wide_of = lambda nm: done['out_' + nm].astype(f32)  14.3 us
  transfers between devices with their start and end apart: 5, of which 4 were waited for; matrix products, arithmetic and copies ran while one was open for 16% of the time, Pallas kernels for 48%

profile of v1, /device:TPU:0, one launch (start us, length us, event | category | flops | bytes accessed | tf_op | source)
XLA Modules:
  0.0 546.3 jit_solution(5819323288205208562)
XLA Ops:
  8.8 1.5 fusion.10
  12.2 0.9 and_convert_fusion
  13.8 1.5 fusion.12.refs_11_
  15.4 2.3 convolution_convert_fusion.3.refs_9_
  17.6 3.2 multiply_convert_fusion.5
  20.8 2.3 copy.100
  23.2 3.5 fusion.20
  28.4 23.2 %all-reduce = bf16[64]{0:T(256)(128)(2,1)S(1)} all-reduce(bf16[64]{0:T(256)(128)(2,1)S(1)} %dynamic-update-slice), channel_id=2, replica_groups=mesh['wide'=8,'narrow'=4] {'wide'}, use_global_device_ids=true, to_apply=%add | all-reduce | flops 64 | bytes 256
  51.7 1.1 fusion.23
  52.8 1.3 fusion.33
  54.0 3.2 multiply_convert_fusion.6
  57.2 7.0 %fusion = f32[8,128,512]{2,1,0:T(8,128)} fusion(f32[512,512]{1,0:T(8,128)} %fusion.33, f32[512,512]{1,0:T(8,128)} %fusion.23, f32[8]{0:T(128)S(1)} %get-tuple-element.166, bf16[512,8,128]{0,2,1:T(8,128)(2,1)} %bitcast.108, bf16[512,1024]{1,0:T(8,128)(2,1)} %get-tuple-element.155.refs_7_, bf16[512,1024]{1,0:T(8,128)(2,1)} %convolution_convert_fusion.3.refs_9_), kind=kOutput, calls=%fused_computation.7 | convolution fusion | flops 1082130432 | bytes 7340064 | tf_op jit(solution)/shard_map/hts,shd->thd/dot_general | solution.py:891
  64.2 14.9 %all-gather.9.cloned.1.call-done = bf16[64,128,128]{2,1,0:T(8,128)(2,1)} async-done(((bf16[8,128,128]{2,1,0:T(8,128)(2,1)}), bf16[64,128,128]{2,1,0:T(8,128)(2,1)}) %all-gather.9.cloned.1.call-update) | async-done | bytes 2097168 | tf_op jit(solution)/shard_map/all_gather | solution.py:787
  79.2 10.7 %while.12 = (s32[]{:T(128)}, f32[8,128,128]{2,1,0:T(8,128)S(1)}, s32[]{:T(128)}, bf16[8,8]{1,0:T(8,128)(2,1)S(1)}, bf16[8,8,128,128]{3,2,1,0:T(8,128)(2,1)}, /*index=5*/s32[]{:T(128)}, s32[]{:T(128)}, s32[]{:T(128)}) while((s32[]{:T(128)}, f32[8,128,128]{2,1,0:T(8,128)S(1)}, s32[]{:T(128)}, bf16[8,8]{1,0:T(8,128)(2,1)S(1)}, ...), condition=%wide.region_4.5_spmd, body=%wide.region_3.4_spmd.sunk | while | flops 393229 | bytes 1310935 | solution.py:802
  90.0 2.9 multiply_reduce_fusion.1
  92.9 1.6 broadcast_multiply_fusion
  94.5 2.9 copy.99
  97.3 6.0 %fusion.39 = (bf16[512,1024]{1,0:T(8,128)(2,1)}, bf16[512,1024]{1,0:T(8,128)(2,1)S(1)}, bf16[512,1024]{1,0:T(8,128)(2,1)}) fusion(f32[512,1024]{1,0:T(8,128)} %copy.99, bf16[512,1024]{1,0:T(8,128)(2,1)} %copy-done.6, bf16[1024,1024]{1,0:T(8,128)(2,1)} %refs_21_.1), kind=kOutput, calls=%fused_computation.75 | convolution fusion | flops 1075838976 | bytes 8388608 | tf_op jit(solution)/shard_map/dot_general | solution.py:888
  103.4 1.4 multiply_reduce_fusion
  104.8 1.3 copy-done.4
  106.1 1.2 multiply_convert_fusion.7
  108.1 40.4 %all-gather.7.cloned.1.call-done = bf16[2048,1024]{1,0:T(8,128)(2,1)} async-done(((bf16[512,1024]{1,0:T(8,128)(2,1)}), bf16[2048,1024]{1,0:T(8,128)(2,1)}) %all-gather.7.cloned.1.call-update) | async-done | bytes 4194320 | tf_op jit(solution)/shard_map/all_gather | solution.py:907
  148.6 8.5 %fusion.43 = f32[2048,704]{0,1:T(8,128)} fusion(bf16[2048,1024]{1,0:T(8,128)(2,1)} %all-gather.7.cloned.1.call-done, bf16[1024,704]{0,1:T(8,128)(2,1)} %param.28), kind=kOutput, calls=%fused_computation.79 | convolution fusion | flops 2952790016 | bytes 11403264 | tf_op jit(solution)/shard_map/dot_general | solution.py:909
  157.0 6.5 %fusion.42 = f32[2048,704]{0,1:T(8,128)} fusion(bf16[2048,1024]{1,0:T(8,128)(2,1)S(1)} %copy-done.19, bf16[1024,704]{0,1:T(8,128)(2,1)} %param.27), kind=kOutput, calls=%fused_computation.78 | convolution fusion | flops 2952790016 | bytes 11403264 | tf_op jit(solution)/shard_map/dot_general | solution.py:908
  163.5 21.1 %all-gather.11.cloned.1.call-done = bf16[1,2048,1024]{2,1,0:T(8,128)(2,1)} async-done(((bf16[1,512,1024]{2,1,0:T(8,128)(2,1)}), bf16[1,2048,1024]{2,1,0:T(8,128)(2,1)}) %all-gather.11.cloned.1.call-update) | async-done | bytes 4194320 | tf_op jit(solution)/shard_map/all_gather | solution.py:919
  184.6 8.7 %multiply_convert_fusion.1 = (bf16[2048,704]{0,1:T(8,128)(2,1)S(1)}, bf16[2048,704]{0,1:T(8,128)(2,1)}, bf16[2048,704]{0,1:T(8,128)(2,1)S(1)}) fusion(f32[2048,704]{0,1:T(8,128)} %fusion.42, f32[2048,704]{0,1:T(8,128)} %fusion.43, bf16[704,1024]{1,0:T(8,128)(2,1)S(1)} %copy-done, bf16[1,2048,1024]{2,1,0:T(8,128)(2,1)} %all-gather.11.cloned.1.call-done), kind=kOutput, calls=%fused_computation.4 | convolution fusion | flops 2961440768 | bytes 25821184 | tf_op jit(solution)/shard_map/dot_general | solution.py:820
  193.4 3.5 fusion.44
  196.9 5.2 add_convert_fusion
  202.6 7.0 %convolution_convert_fusion = bf16[2048,1024]{1,0:T(8,128)(2,1)} fusion(bf16[2048,704]{0,1:T(8,128)(2,1)} %get-tuple-element.150, bf16[704,1024]{1,0:T(8,128)(2,1)S(1)} %copy-done), kind=kOutput, calls=%fused_computation.15 | convolution fusion | flops 2954887168 | bytes 8519680 | tf_op jit(solution)/shard_map/dot_general | solution.py:912
  211.2 6.6 %convolution_convert_fusion.2 = bf16[1024,704]{0,1:T(8,128)(2,1)S(1)} fusion(bf16[2048,704]{0,1:T(8,128)(2,1)} %copy-done.3, bf16[2048,1024]{1,0:T(8,128)(2,1)} %all-gather.7.cloned.1.call-done), kind=kOutput, calls=%fused_computation.41 | convolution fusion | flops 2953510912 | bytes 8519680 | tf_op jit(solution)/shard_map/dot_general | solution.py:814
  217.8 1.6 copy.94.refs_16_
  219.4 6.9 %convolution_convert_fusion.1 = bf16[1024,704]{0,1:T(8,128)(2,1)S(1)} fusion(bf16[2048,704]{0,1:T(8,128)(2,1)} %copy-done.2, bf16[2048,1024]{1,0:T(8,128)(2,1)} %all-gather.7.cloned.1.call-done), kind=kOutput, calls=%fused_computation.40 | convolution fusion | flops 2953510912 | bytes 8519680 | tf_op jit(solution)/shard_map/dot_general | solution.py:814
  226.3 1.6 copy.95.refs_17_
  227.8 7.4 %fusion.17.refs_15_ = bf16[704,1024]{1,0:T(8,128)(2,1)} fusion(bf16[2048,704]{0,1:T(8,128)(2,1)} %get-tuple-element.150, bf16[1,2048,1024]{2,1,0:T(8,128)(2,1)} %all-gather.11.cloned.1.call-done), kind=kOutput, calls=%fused_computation.39 | convolution fusion | flops 2953510912 | bytes 8519680 | tf_op jit(solution)/shard_map/dot_general | solution.py:814
  235.2 11.6 %reduce-scatter.5.cloned.1.call-done = bf16[512,1024]{1,0:T(8,128)(2,1)} async-done(((bf16[2048,1024]{1,0:T(8,128)(2,1)}), bf16[512,1024]{1,0:T(8,128)(2,1)}) %reduce-scatter.5.cloned.1.call-update) | async-done | bytes 1048592 | tf_op jit(solution)/shard_map/reduce_scatter | solution.py:926
  246.8 2.8 convert_element_type.193.refs_0_
  249.6 263.2 %attention_backward.1 = (bf16[1024,1024]{1,0:T(8,128)(2,1)}, bf16[1024,1024]{1,0:T(8,128)(2,1)}, bf16[1024,1024]{1,0:T(8,128)(2,1)}, bf16[1024,1024]{1,0:T(8,128...) custom-call(f32[512,1024]{1,0:T(8,128)} %convert_element_type.193.re, ...), custom_call_target="tpu_custom_call" | custom-call | flops 20000000000 | bytes 40000000 | tf_op jit(solution)/shard_map/attention_backward/pallas_call | solution.py:33
  512.8 3.1 copy.96
  515.9 2.1 copy.97
  518.1 1.9 convert_element_type.210
  520.3 2.5 convert_element_type.203
  522.7 2.5 convert_element_type.204
  525.2 2.5 convert_element_type.205
  527.7 2.5 convert_element_type.206
  530.2 2.5 convert_element_type.207
  532.7 1.4 fusion.40
  534.1 3.3 fusion.24
  537.4 1.3 copy.130
  (86 shorter events, 8.0 us)
Async XLA Ops:
  7.2 177.5 %copy-start = (bf16[704,1024]{1,0:T(8,128)(2,1)S(1)}, bf16[704,1024]{1,0:T(8,128)(2,1)}, u32[]{:S(2)}) copy-start(bf16[704,1024]{1,0:T(8,128)(2,1)} %param.29) | copy-start | bytes 4325380
  7.2 72.0 %all-gather.9.cloned.1.call-start = ((), (), s32[]{:S(2)}) async-start(), calls=%async_computation.5 | async-start | bytes 2359296 | tf_op jit(solution)/shard_map/all_gather | solution.py:787
  12.2 3.2 copy-start.21
  15.4 38.7 %copy-start.6 = (bf16[512,1024]{1,0:T(8,128)(2,1)}, bf16[512,1024]{1,0:T(8,128)(2,1)S(1)}, u32[]{:S(2)}) copy-start(bf16[512,1024]{1,0:T(8,128)(2,1)S(1)} %fusion.12.refs_11_) | copy-start | bytes 3145732
  15.4 2.3 copy-start.20
  20.8 2.3 copy-start.18
  23.1 3.8 copy-start.26
  26.8 121.8 %all-gather.7.cloned.1.call-start = ((), (), s32[]{:S(2)}) async-start(), calls=%async_computation.2 | async-start | bytes 5242880 | tf_op jit(solution)/shard_map/all_gather | solution.py:907
  51.7 2.4 copy-start.22
  79.2 10.8 %copy-start.15 = (bf16[512,1024]{1,0:T(8,128)(2,1)S(1)}, bf16[512,1024]{1,0:T(8,128)(2,1)}, u32[]{:S(2)}) copy-start(bf16[512,1024]{1,0:T(8,128)(2,1)} %get-tuple-element.155.refs_7_) | copy-start | bytes 3145732
  97.3 6.0 %copy-start.5 = (bf16[1,512,1024]{2,1,0:T(8,128)(2,1)S(1)}, bf16[1,512,1024]{2,1,0:T(8,128)(2,1)}, u32[]{:S(2)}) copy-start(bf16[1,512,1024]{2,1,0:T(8,128)(2,1)} %param.16) | copy-start | bytes 3145732
  97.3 6.0 %copy-start.23 = (bf16[1024,1024]{1,0:T(8,128)(2,1)S(1)}, bf16[1024,1024]{1,0:T(8,128)(2,1)}, u32[]{:S(2)}) copy-start(bf16[1024,1024]{1,0:T(8,128)(2,1)} %refs_3_.1) | copy-start | bytes 6291460
  103.4 1.4 copy-start.16
  103.4 2.7 copy-start.17
  104.8 1.3 copy-start.4
  107.3 77.3 %all-gather.11.cloned.1.call-start = ((), (), s32[]{:S(2)}) async-start(), calls=%async_computation.6 | async-start | bytes 5242880 | tf_op jit(solution)/shard_map/all_gather | solution.py:919
  108.1 138.8 %reduce-scatter.5.cloned.1.call-start = ((), (), s32[]{:S(2)}) async-start(), calls=%async_computation.4 | async-start | bytes 5242880 | tf_op jit(solution)/shard_map/reduce_scatter | solution.py:926
  148.6 8.5 %copy-start.19 = (bf16[2048,1024]{1,0:T(8,128)(2,1)S(1)}, bf16[2048,1024]{1,0:T(8,128)(2,1)}, u32[]{:S(2)}) copy-start(bf16[2048,1024]{1,0:T(8,128)(2,1)} %all-gather.7.cloned.1.call-done) | copy-start | bytes 12582916
  184.6 8.7 %copy-start.24 = (bf16[1024,704]{0,1:T(8,128)(2,1)S(1)}, bf16[1024,704]{0,1:T(8,128)(2,1)}, u32[]{:S(2)}) copy-start(bf16[1024,704]{0,1:T(8,128)(2,1)} %param.27) | copy-start | bytes 4325380
  193.4 3.5 copy-start.3
  193.4 3.5 copy-start.2
  193.4 3.5 copy-start.25
  202.2 331.9 %reduce-scatter.3.cloned.1.call-start = ((), (), s32[]{:S(2)}) async-start(), calls=%async_computation.3 | async-start | bytes 5242880 | tf_op jit(solution)/shard_map/reduce_scatter | solution.py:911
  512.8 3.1 copy-start.13
  515.9 2.2 copy-start.14
  518.1 2.2 copy-start.11
  520.3 2.5 copy-start.10
  522.7 2.5 copy-start.9
  525.2 2.5 copy-start.8
  527.7 2.5 copy-start.7
  534.1 3.3 copy-start.12
  537.4 2.1 copy-start.1
Sparse Core Ops, SparseCore 0:
  26.9 52.2 all-gather.8
  107.5 41.0 all-gather.6
  150.1 34.4 all-gather.10
  202.3 44.5 reduce-scatter.4
  249.4 62.0 reduce-scatter.2
